TPU v7x, 512 devices: a whole 4x8x8 slice. The times are simulated.
512 devices in a mesh: seq: 128 (over z, y, core), mp: 4 (over x).
Axes of the slice: x: 4, y: 8, z: 8, core: 2. Of those that a mesh axis runs over, the one named last changes fastest.
Arguments:
- x_in: bfloat16 [16384, 8192], P('seq', 'mp'), may hold values from -6 to 6
- bc_in: bfloat16 [16384, 2, 1024], P('seq', None, 'mp'), may hold values from -4 to 4
- dt_raw: bfloat16 [16384, 128], P('seq', 'mp'), may hold values from -4 to 4
- doc_id: int32 [16384], P('seq'), may hold values from 0 to 4, as said below
- conv_x: float32 [4, 8192], P(None, 'mp'), may hold values from -3 to 3
- bias_x: float32 [8192], P('mp'), may hold values from -3 to 3
- conv_bc: float32 [4, 2, 1024], P(None, None, 'mp'), may hold values from -3 to 3
- bias_bc: float32 [2, 1024], P(None, 'mp'), may hold values from -3 to 3
- rate: float32 [128], P('mp'), may hold values from 2e-05 to 0.1
- dskip: float32 [128], P('mp'), may hold values from 0.5 to 4
- z_in: bfloat16 [16384, 8192], P('seq', 'mp'), may hold values from -6 to 6
- norm_gain: float32 [8192], P('mp'), may hold values from 0.1 to 1.9
Outputs:
- mixed: bfloat16 [16384, 8192], P('seq', 'mp')
Inputs may be any that keep to these rules, and one draw needn't show every extreme that they name: doc_id of storage row i names the document of position p(i); along positions it starts at 0 and rises by 0 or 1 from one position to the next; the window holds 5 documents.
All inputs are finite; a program needn't handle non-finite values.
Results may differ from a plain program's by a relative error of at most 0.009.
Values may be sent and summed in bfloat16 or wider, within the bound.
A program may use at most 64 MiB of HBM per device.

v0:
```python
import jax
import jax.numpy as jnp
from jax import lax
from jax.sharding import PartitionSpec as P

DSTATE = 128
SPAN = 256
DI = 8192


EPSILON = 1e-05


def from_behind(block, axis, distance):
    devices = range(lax.axis_size(axis))
    route = [((i - distance) % len(devices), i) for i in devices]
    return lax.ppermute(block, axis, route)


def from_behind_2(value, axis, by):
    peers = lax.axis_size(axis)
    pairs = [(i, i + by) for i in range(peers) if 0 <= i + by < peers]
    return lax.ppermute(value, axis, pairs)


def conv_runs(extended, extended_docs, weight, bias, tap_count):
    row_count = extended.shape[1] - tap_count + 1
    own_docs = extended_docs[:, tap_count - 1 :]
    total = jnp.zeros((extended.shape[0], row_count, extended.shape[2]), jnp.float32) + bias
    for offset in range(tap_count):
        same_doc = (extended_docs[:, offset : offset + row_count] == own_docs).astype(jnp.float32)[
            :, :, None
        ]
        total = (
            total
            + weight[offset]
            * extended[:, offset : offset + row_count].astype(jnp.float32)
            * same_doc
        )
    return jax.nn.silu(total).astype(jnp.bfloat16)


def span_terms(x_spans, b_spans, c_spans, step_size, head_rate, span_docs):
    size = span_docs.shape[1]
    decay_sum = jnp.cumsum(-step_size * head_rate, axis=1)
    scores = jnp.einsum("cin,cjn->cij", c_spans, b_spans, preferred_element_type=jnp.float32)
    row_index = lax.broadcasted_iota(jnp.int32, (size, size), 0)
    col_index = lax.broadcasted_iota(jnp.int32, (size, size), 1)
    visible = (span_docs[:, :, None] == span_docs[:, None, :]) & (row_index >= col_index)
    visible = visible[..., None]
    spread = jnp.where(visible, decay_sum[:, :, None, :] - decay_sum[:, None, :, :], 0.0)
    mixing = jnp.where(
        visible, scores[..., None] * jnp.exp(spread) * step_size[:, None, :, :], 0.0
    ).astype(jnp.bfloat16)
    inner = jnp.einsum("cijh,cjhp->cihp", mixing, x_spans, preferred_element_type=jnp.float32)
    last_doc = span_docs[:, -1:]
    tail_weight = (
        jnp.exp(decay_sum[:, -1:, :] - decay_sum)
        * step_size
        * (span_docs == last_doc).astype(jnp.float32)[:, :, None]
    )
    weighted = (b_spans.astype(jnp.float32)[:, :, None, :] * tail_weight[..., None]).astype(
        jnp.bfloat16
    )
    states = jnp.einsum("cjhn,cjhp->chnp", weighted, x_spans, preferred_element_type=jnp.float32)
    through = jnp.exp(decay_sum[:, -1, :]) * (span_docs[:, :1] == last_doc).astype(jnp.float32)
    return (inner, decay_sum, (states, through, span_docs[:, :1], last_doc))


def outputs(x_spans, c_spans, head_skip, inner, decay_sum, span_docs, incoming, incoming_doc):
    cross = jnp.einsum(
        "cin,chnp->cihp", c_spans, incoming.astype(jnp.bfloat16), preferred_element_type=jnp.float32
    )
    scale = (
        jnp.exp(decay_sum) * (span_docs == incoming_doc[:, None]).astype(jnp.float32)[:, :, None]
    )
    return inner + cross * scale[..., None] + head_skip[:, None] * x_spans.astype(jnp.float32)


def link(earlier, later):
    same_doc = (earlier[3] == later[2]).astype(jnp.float32)
    passed = later[1] * same_doc
    return (
        later[0] + passed[..., None, None] * earlier[0],
        passed * earlier[1],
        earlier[2],
        later[3],
    )


def local(
    x_in, bc_in, dt_raw, doc_id, conv_x, bias_x, conv_bc, bias_bc, rate, dskip, z_in, norm_gain
):
    seq_count = lax.axis_size("seq")
    tok_dev, width = x_in.shape
    heads_mp = rate.shape[0]
    head_dim = width // heads_mp
    tap_count = conv_x.shape[0]
    margin = tap_count - 1
    bc_width = bc_in.shape[2]
    groups_mp = bc_width // DSTATE
    run_count = 2 * max(1, 2 * seq_count // heads_mp)
    run_len = tok_dev // run_count
    seg_count = run_count // 2
    sub_count = run_count // seg_count
    pieces = seq_count // seg_count
    per_dev = heads_mp // pieces
    seg_len = sub_count * seq_count * run_len
    x_runs = x_in.reshape(run_count, run_len, width)
    bc_runs = bc_in.reshape(run_count, run_len, 2 * bc_width)
    doc_runs = doc_id.reshape(run_count, run_len)
    received = from_behind(
        (x_runs[:, -margin:], bc_runs[:, -margin:], doc_runs[:, -margin:]), "seq", 1
    )
    first_device = lax.axis_index("seq") == 0

    def settle(piece):
        moved = jnp.concatenate([jnp.zeros_like(piece[:1]), piece[:-1]], axis=0)
        return jnp.where(first_device, moved, piece)

    rim_x, rim_bc, rim_docs = (settle(received[0]), settle(received[1]), settle(received[2]))
    extended_docs = jnp.concatenate([rim_docs, doc_runs], axis=1)
    x_conv = conv_runs(
        jnp.concatenate([rim_x, x_runs], axis=1), extended_docs, conv_x, bias_x, tap_count
    )
    bc_conv = conv_runs(
        jnp.concatenate([rim_bc, bc_runs], axis=1),
        extended_docs,
        conv_bc.reshape(tap_count, 2 * bc_width),
        bias_bc.reshape(2 * bc_width),
        tap_count,
    )
    x_send = x_conv.reshape(seg_count, sub_count, run_len, pieces, per_dev * head_dim)
    x_send = x_send.transpose(0, 3, 1, 2, 4).reshape(
        seq_count, sub_count, run_len, per_dev * head_dim
    )
    bc_send = jnp.repeat(
        bc_conv.reshape(run_count, run_len, 2, groups_mp, DSTATE), pieces // groups_mp, axis=3
    )
    bc_send = bc_send.reshape(seg_count, sub_count, run_len, 2, pieces, DSTATE).transpose(
        0, 4, 1, 2, 3, 5
    )
    bc_send = bc_send.reshape(seq_count, sub_count, run_len, 2 * DSTATE)
    dt_send = dt_raw.reshape(seg_count, sub_count, run_len, pieces, per_dev).transpose(
        0, 3, 1, 2, 4
    )
    dt_send = dt_send.reshape(seq_count, sub_count, run_len, per_dev)
    doc_send = jnp.broadcast_to(
        doc_id.reshape(seg_count, 1, sub_count, run_len), (seg_count, pieces, sub_count, run_len)
    )
    doc_send = doc_send.reshape(seq_count, sub_count, run_len)
    arrived = (
        lax.all_to_all(x_send, "seq", split_axis=0, concat_axis=0, tiled=True),
        lax.all_to_all(bc_send, "seq", split_axis=0, concat_axis=0, tiled=True),
        lax.all_to_all(dt_send, "seq", split_axis=0, concat_axis=0, tiled=True),
        lax.all_to_all(doc_send, "seq", split_axis=0, concat_axis=0, tiled=True),
    )

    def segment_rows(array):
        return jnp.swapaxes(array, 0, 1).reshape((seg_len,) + array.shape[3:])

    x_segment = segment_rows(arrived[0])
    bc_segment = segment_rows(arrived[1])
    dt_segment = segment_rows(arrived[2])
    doc_segment = segment_rows(arrived[3])
    piece_index = lax.axis_index("seq") % pieces
    head_rate = lax.dynamic_index_in_dim(
        rate.reshape(pieces, per_dev), piece_index, 0, keepdims=False
    )
    head_skip = lax.dynamic_index_in_dim(
        dskip.reshape(pieces, per_dev), piece_index, 0, keepdims=False
    )
    span_count = seg_len // SPAN
    x_spans = x_segment.reshape(span_count, SPAN, per_dev, head_dim)
    b_spans = bc_segment[:, :DSTATE].reshape(span_count, SPAN, DSTATE)
    c_spans = bc_segment[:, DSTATE:].reshape(span_count, SPAN, DSTATE)
    step_size = jax.nn.softplus(dt_segment.astype(jnp.float32)).reshape(span_count, SPAN, per_dev)
    span_docs = doc_segment.reshape(span_count, SPAN)
    inner, decay_sum, summary = span_terms(
        x_spans, b_spans, c_spans, step_size, head_rate, span_docs
    )
    running = lax.associative_scan(link, summary, axis=0)
    segment_total = jax.tree.map(lambda leaf: leaf[-1], running)

    def advance(turn, prefix_now):
        return from_behind_2(link(prefix_now, segment_total), "seq", pieces)

    prefix = lax.fori_loop(0, seg_count - 1, advance, jax.tree.map(jnp.zeros_like, segment_total))
    prior_state, prior_doc = (prefix[0], prefix[3])
    earlier = jax.tree.map(lambda leaf: leaf[:-1], running)
    local_in = jnp.concatenate([jnp.zeros_like(earlier[0][:1]), earlier[0]], axis=0)
    factor = jnp.concatenate(
        [
            jnp.ones((1, per_dev), jnp.float32),
            earlier[1] * (prior_doc == earlier[2]).astype(jnp.float32),
        ],
        axis=0,
    )
    incoming = local_in + factor[:, :, None, None] * prior_state[None]
    incoming_doc = jnp.concatenate([prior_doc, earlier[3][:, 0]], axis=0)
    y_rows = outputs(
        x_spans, c_spans, head_skip, inner, decay_sum, span_docs, incoming, incoming_doc
    )
    y_rows = y_rows.reshape(seg_len, per_dev * head_dim).astype(jnp.bfloat16)
    y_send = jnp.swapaxes(y_rows.reshape(sub_count, seq_count, run_len, per_dev * head_dim), 0, 1)
    returned = lax.all_to_all(y_send, "seq", split_axis=0, concat_axis=0, tiled=True)
    y_local = returned.reshape(seg_count, pieces, sub_count, run_len, per_dev * head_dim)
    y_local = y_local.transpose(0, 2, 3, 1, 4).reshape(tok_dev, width)
    gated = y_local.astype(jnp.float32) * jax.nn.silu(z_in.astype(jnp.float32))
    square = lax.psum(jnp.sum(gated * gated, axis=1), "mp")
    return (gated * lax.rsqrt(square / DI + EPSILON)[:, None] * norm_gain).astype(jnp.bfloat16)


def solution(mesh):
    placed = (
        P("seq", "mp"),
        P("seq", None, "mp"),
        P("seq", "mp"),
        P("seq"),
        P(None, "mp"),
        P("mp"),
        P(None, None, "mp"),
        P(None, "mp"),
        P("mp"),
        P("mp"),
        P("seq", "mp"),
        P("mp"),
    )
    return jax.shard_map(
        local, mesh=mesh, in_specs=placed, out_specs=P("seq", "mp"), check_vma=False
    )
```

profile of v0, /device:TPU:1, one launch (start us, length us, event | category | flops | bytes accessed | tf_op | source)
XLA Modules:
  0.0 245.7 jit_solution(226000129790184515)
XLA Ops:
  0.0 0.9 reshape.212
  0.9 0.8 copy.173
  1.6 18.4 %all-to-all-start.3 = ((bf16[128,2,8,2]{2,3,1,0:T(2,128)(2,1)}), bf16[128,2,8,2]{2,3,1,0:T(2,128)(2,1)S(1)}, u32[]{:S(2)}, u32[]{:S(2)}) async-start(bf16[128,2,8,2]{2,3,1,0:T(2,128)(2,1)} %bitcast.19), calls=%async_computation.3 | async-start | bytes 262144 | tf_op jit(solution)/shard_map/all_to_all | solution.py:155
  20.9 3.5 %collective-permute-start.2 = (s32[16,3]{1,0:T(8,128)S(1)}, s32[16,3]{1,0:T(8,128)S(1)}, u32[]{:S(2)}, u32[]{:S(2)}) collective-permute-start(s32[16,3]{1,0:T(8,128)S(1)} %slice.378), channel_id=1, source_target_pairs={{508,0},{0,4},{4,8},{8,12},{12,16},{16,20},{20,24},{24,28},{28,32}... | collective-permute-start | bytes 584 | tf_op jit(solution)/shard_map/ppermute | solution.py:17
  24.4 1.0 reshape.206
  25.5 2.1 collective-permute-start.3
  27.6 1.2 slice.374
  28.8 3.3 %collective-permute-start.1 = (bf16[16,3,2048]{2,1,0:T(4,128)(2,1)S(1)}, bf16[16,3,2048]{2,1,0:T(4,128)(2,1)S(1)}, u32[]{:S(2)}, u32[]{:S(2)}) collective-permute-start(bf16[16,3,2048]{2,1,0:T(4,128)(2,1)S(1)} %slice.374), channel_id=1, source_target_pairs={{508,0},{0,4},{4,8},{8,12},{12,16},{16,20},{20,24},{24,28},{28,32}... | collective-permute-start | bytes 589832 | tf_op jit(solution)/shard_map/ppermute | solution.py:17
  32.2 0.7 broadcast_in_dim.20
  33.7 0.7 reshape.217
  35.2 0.9 fusion.41
  37.7 11.5 %all-to-all-start.1 = ((s32[128,2,8]{2,1,0:T(2,128)}), s32[128,2,8]{2,1,0:T(2,128)S(1)}, u32[]{:S(2)}, u32[]{:S(2)}) async-start(s32[128,2,8]{2,1,0:T(2,128)} %bitcast.9), calls=%async_computation.1 | async-start | bytes 262144 | tf_op jit(solution)/shard_map/all_to_all | solution.py:156
  49.6 1.1 reduce-window.6
  51.1 10.8 %all-to-all-done.1 = s32[128,2,8]{2,1,0:T(2,128)S(1)} async-done(((s32[128,2,8]{2,1,0:T(2,128)}), s32[128,2,8]{2,1,0:T(2,128)S(1)}, u32[]{:S(2)}, u32[]{:S(2)}) %all-to-all-start.1) | async-done | bytes 8224 | tf_op jit(solution)/shard_map/all_to_all | solution.py:156
  65.6 1.2 pad_add_fusion.8
  69.0 1.2 fusion.20
  70.2 0.9 copy.144
  71.0 5.6 %all-to-all-start = ((bf16[128,2,8,128]{3,2,1,0:T(8,128)(2,1)}), bf16[128,2,8,128]{3,2,1,0:T(8,128)(2,1)S(1)}, u32[]{:S(2)}, u32[]{:S(2)}) async-start(bf16[128,2,8,128]{3,2,1,0:T(8,128)(2,1)} %bitcast.7), calls=%async_computation | async-start | bytes 1048576 | tf_op jit(solution)/shard_map/all_to_all | solution.py:153
  78.5 1.4 copy.147
  79.9 17.4 %all-to-all-done = bf16[128,2,8,128]{3,2,1,0:T(8,128)(2,1)S(1)} async-done(((bf16[128,2,8,128]{3,2,1,0:T(8,128)(2,1)}), bf16[128,2,8,128]{3,2,1,0:T(8,128)(2,1)S(1)}, u32[]{:S(2)}, u32[]{:S(2)}) %all-to-all-start) | async-done | bytes 524320 | tf_op jit(solution)/shard_map/all_to_all | solution.py:153
  97.3 5.5 %all-to-all-start.2 = ((bf16[128,2,8,256]{3,2,1,0:T(8,128)(2,1)}), bf16[128,2,8,256]{3,2,1,0:T(8,128)(2,1)S(1)}, u32[]{:S(2)}, u32[]{:S(2)}) async-start(bf16[128,2,8,256]{3,2,1,0:T(8,128)(2,1)} %bitcast.13), calls=%async_computation.2 | async-start | bytes 2097152 | tf_op jit(solution)/shard_map/all_to_all | solution.py:154
  104.3 1.2 pad_add_fusion.4
  106.3 1.3 pad_add_fusion.5
  110.6 3.8 %collective-permute-start.4 = (s32[1]{0:T(128)}, s32[1]{0:T(128)}, u32[]{:S(2)}, u32[]{:S(2)}) collective-permute-start(s32[1]{0:T(128)} %bitcast.31), channel_id=1, source_target_pairs={{0,64},{4,68},{8,72},{12,76},{16,80},{20,84},{24,88},{28,92},{32,9... | collective-permute-start | bytes 20 | tf_op jit(solution)/shard_map/while/body/eval_jaxpr/ppermute | solution.py:23
  114.8 1.2 compare_and_fusion
  117.1 16.5 %all-to-all-done.2 = bf16[128,2,8,256]{3,2,1,0:T(8,128)(2,1)S(1)} async-done(((bf16[128,2,8,256]{3,2,1,0:T(8,128)(2,1)}), bf16[128,2,8,256]{3,2,1,0:T(8,128)(2,1)S(1)}, u32[]{:S(2)}, u32[]{:S(2)}) %all-to-all-start.2) | async-done | bytes 1048608 | tf_op jit(solution)/shard_map/all_to_all | solution.py:154
  133.9 1.0 fusion.15
  135.6 3.2 %pad.88 = f32[8,2,128,64]{2,3,1,0:T(8,128)} pad(f32[4,2,128,64]{2,3,1,0:T(8,128)S(1)} %add.225, f32[]{:T(128)} %constant.57.clone.1), padding=1_0_1x0_0_0x0_0_0x0_0_0 | pad | bytes 786436 | tf_op jit(solution)/shard_map/pad | solution.py:182
  138.9 46.7 %while.14 = (s32[]{:T(128)}, f32[2,128,64]{2,1,0:T(8,128)S(1)}, s32[1]{0:T(128)}, s32[1]{0:T(128)}, f32[2]{0:T(128)S(1)}, /*index=5*/f32[2,128,64]{2,1,0:T(8,128)S(1)}, s32[1]{0:T(128)}, s32[]{:T(128)}) while((s32[]{:T(128)}, f32[2,128,64]{2,1,0:T(8,128)S(1)}, s32[1]{0:T(128)}, s32[1]{0:T(128)}, f32[2]{0:T(128)S(1)}, ...), condition=%wide.region_3.4_spmd, body=%wide.region_2.3_spmd.sunk | while | flops 32774 | bytes 458927 | solution.py:188
  139.7 2.3 collective-permute-start
  142.6 2.0 collective-permute-done
  145.3 4.1 %collective-permute-start = (f32[2,128,64]{2,1,0:T(8,128)S(1)}, f32[2,128,64]{2,1,0:T(8,128)S(1)}, u32[]{:S(2)}, u32[]{:S(2)}) collective-permute-start(f32[2,128,64]{2,1,0:T(8,128)S(1)} %multiply_add_fusion.4), channel_id=1, source_target_pairs={{0,64},{4,68},{8,72},{12,76},{16,80},{20,84},{24,88},{28,92},{32,9... | collective-permute-start | bytes 196616 | tf_op jit(solution)/shard_map/while/body/eval_jaxpr/ppermute | solution.py:23
  150.1 1.3 collective-permute-done
  152.1 3.8 %collective-permute-start = (f32[2,128,64]{2,1,0:T(8,128)S(1)}, f32[2,128,64]{2,1,0:T(8,128)S(1)}, u32[]{:S(2)}, u32[]{:S(2)}) collective-permute-start(f32[2,128,64]{2,1,0:T(8,128)S(1)} %multiply_add_fusion.4), channel_id=1, source_target_pairs={{0,64},{4,68},{8,72},{12,76},{16,80},{20,84},{24,88},{28,92},{32,9... | collective-permute-start | bytes 196616 | tf_op jit(solution)/shard_map/while/body/eval_jaxpr/ppermute | solution.py:23
  156.5 1.3 collective-permute-done
  158.5 3.8 %collective-permute-start = (f32[2,128,64]{2,1,0:T(8,128)S(1)}, f32[2,128,64]{2,1,0:T(8,128)S(1)}, u32[]{:S(2)}, u32[]{:S(2)}) collective-permute-start(f32[2,128,64]{2,1,0:T(8,128)S(1)} %multiply_add_fusion.4), channel_id=1, source_target_pairs={{0,64},{4,68},{8,72},{12,76},{16,80},{20,84},{24,88},{28,92},{32,9... | collective-permute-start | bytes 196616 | tf_op jit(solution)/shard_map/while/body/eval_jaxpr/ppermute | solution.py:23
  163.0 1.3 collective-permute-done
  165.0 3.8 %collective-permute-start = (f32[2,128,64]{2,1,0:T(8,128)S(1)}, f32[2,128,64]{2,1,0:T(8,128)S(1)}, u32[]{:S(2)}, u32[]{:S(2)}) collective-permute-start(f32[2,128,64]{2,1,0:T(8,128)S(1)} %multiply_add_fusion.4), channel_id=1, source_target_pairs={{0,64},{4,68},{8,72},{12,76},{16,80},{20,84},{24,88},{28,92},{32,9... | collective-permute-start | bytes 196616 | tf_op jit(solution)/shard_map/while/body/eval_jaxpr/ppermute | solution.py:23
  169.4 1.3 collective-permute-done
  171.4 4.1 %collective-permute-start = (f32[2,128,64]{2,1,0:T(8,128)S(1)}, f32[2,128,64]{2,1,0:T(8,128)S(1)}, u32[]{:S(2)}, u32[]{:S(2)}) collective-permute-start(f32[2,128,64]{2,1,0:T(8,128)S(1)} %multiply_add_fusion.4), channel_id=1, source_target_pairs={{0,64},{4,68},{8,72},{12,76},{16,80},{20,84},{24,88},{28,92},{32,9... | collective-permute-start | bytes 196616 | tf_op jit(solution)/shard_map/while/body/eval_jaxpr/ppermute | solution.py:23
  176.2 1.3 collective-permute-done
  178.3 5.4 %collective-permute-start = (f32[2,128,64]{2,1,0:T(8,128)S(1)}, f32[2,128,64]{2,1,0:T(8,128)S(1)}, u32[]{:S(2)}, u32[]{:S(2)}) collective-permute-start(f32[2,128,64]{2,1,0:T(8,128)S(1)} %multiply_add_fusion.4), channel_id=1, source_target_pairs={{0,64},{4,68},{8,72},{12,76},{16,80},{20,84},{24,88},{28,92},{32,9... | collective-permute-start | bytes 196616 | tf_op jit(solution)/shard_map/while/body/eval_jaxpr/ppermute | solution.py:23
  184.3 1.3 collective-permute-done
  187.9 1.6 fusion.10
  189.5 0.8 copy.170
  190.9 43.3 %all_to_all.25 = bf16[128,2,8,128]{3,2,1,0:T(8,128)(2,1)S(1)} all-to-all(bf16[128,2,8,128]{3,2,1,0:T(8,128)(2,1)S(1)} %copy.171), channel_id=1, replica_groups=mesh['seq'=128,'mp'=4] {'seq'}, dimensions={0} | all-to-all | bytes 1048576 | tf_op jit(solution)/shard_map/all_to_all | solution.py:206
  235.8 8.5 %psum.7 = f32[128]{0:T(128)S(1)} all-reduce(f32[128]{0:T(128)S(1)} %multiply_reduce_fusion), channel_id=1, replica_groups=mesh['seq'=128,'mp'=4] {'mp'}, use_global_device_ids=true, to_apply=%region_5.6 | all-reduce | flops 128 | bytes 1024 | tf_op jit(solution)/shard_map/psum | solution.py:210
  244.3 1.4 multiply_convert_fusion.2
  (177 shorter events, 22.5 us)
Async XLA Ops:
  1.6 35.3 %all-to-all-start.3 = ((bf16[128,2,8,2]{2,3,1,0:T(2,128)(2,1)}), bf16[128,2,8,2]{2,3,1,0:T(2,128)(2,1)S(1)}, u32[]{:S(2)}, u32[]{:S(2)}) async-start(bf16[128,2,8,2]{2,3,1,0:T(2,128)(2,1)} %bitcast.19), calls=%async_computation.3 | async-start | bytes 262144 | tf_op jit(solution)/shard_map/all_to_all | solution.py:155
  20.9 16.0 %collective-permute-start.2 = (s32[16,3]{1,0:T(8,128)S(1)}, s32[16,3]{1,0:T(8,128)S(1)}, u32[]{:S(2)}, u32[]{:S(2)}) collective-permute-start(s32[16,3]{1,0:T(8,128)S(1)} %slice.378), channel_id=1, source_target_pairs={{508,0},{0,4},{4,8},{8,12},{12,16},{16,20},{20,24},{24,28},{28,32}... | collective-permute-start | bytes 584 | tf_op jit(solution)/shard_map/ppermute | solution.py:17
  25.5 52.3 %collective-permute-start.3 = (bf16[16,3,512]{2,1,0:T(4,128)(2,1)S(1)}, bf16[16,3,512]{2,1,0:T(4,128)(2,1)S(1)}, u32[]{:S(2)}, u32[]{:S(2)}) collective-permute-start(bf16[16,3,512]{2,1,0:T(4,128)(2,1)S(1)} %slice.386), channel_id=1, source_target_pairs={{508,0},{0,4},{4,8},{8,12},{12,16},{16,20},{20,24},{24,28},{28,32}... | collective-permute-start | bytes 147464 | tf_op jit(solution)/shard_map/ppermute | solution.py:17
  27.5 41.4 %copy-start.2 = (bf16[128,2048]{1,0:T(8,128)(2,1)S(1)}, bf16[128,2048]{1,0:T(8,128)(2,1)}, u32[]{:S(2)}) copy-start(bf16[128,2048]{1,0:T(8,128)(2,1)} %param.14) | copy-start | bytes 1572868
  27.6 41.4 %copy-start.4 = (f32[2048]{0:T(1024)S(1)}, f32[2048]{0:T(1024)}, u32[]{:S(2)}) copy-start(f32[2048]{0:T(1024)} %param.19) | copy-start | bytes 24580
  28.8 39.8 %collective-permute-start.1 = (bf16[16,3,2048]{2,1,0:T(4,128)(2,1)S(1)}, bf16[16,3,2048]{2,1,0:T(4,128)(2,1)S(1)}, u32[]{:S(2)}, u32[]{:S(2)}) collective-permute-start(bf16[16,3,2048]{2,1,0:T(4,128)(2,1)S(1)} %slice.374), channel_id=1, source_target_pairs={{508,0},{0,4},{4,8},{8,12},{12,16},{16,20},{20,24},{24,28},{28,32}... | collective-permute-start | bytes 589832 | tf_op jit(solution)/shard_map/ppermute | solution.py:17
  37.7 24.2 %all-to-all-start.1 = ((s32[128,2,8]{2,1,0:T(2,128)}), s32[128,2,8]{2,1,0:T(2,128)S(1)}, u32[]{:S(2)}, u32[]{:S(2)}) async-start(s32[128,2,8]{2,1,0:T(2,128)} %bitcast.9), calls=%async_computation.1 | async-start | bytes 262144 | tf_op jit(solution)/shard_map/all_to_all | solution.py:156
  71.0 26.3 %all-to-all-start = ((bf16[128,2,8,128]{3,2,1,0:T(8,128)(2,1)}), bf16[128,2,8,128]{3,2,1,0:T(8,128)(2,1)S(1)}, u32[]{:S(2)}, u32[]{:S(2)}) async-start(bf16[128,2,8,128]{3,2,1,0:T(8,128)(2,1)} %bitcast.7), calls=%async_computation | async-start | bytes 1048576 | tf_op jit(solution)/shard_map/all_to_all | solution.py:153
  97.3 36.3 %all-to-all-start.2 = ((bf16[128,2,8,256]{3,2,1,0:T(8,128)(2,1)}), bf16[128,2,8,256]{3,2,1,0:T(8,128)(2,1)S(1)}, u32[]{:S(2)}, u32[]{:S(2)}) async-start(bf16[128,2,8,256]{3,2,1,0:T(8,128)(2,1)} %bitcast.13), calls=%async_computation.2 | async-start | bytes 2097152 | tf_op jit(solution)/shard_map/all_to_all | solution.py:154
  110.6 28.3 %collective-permute-start.4 = (s32[1]{0:T(128)}, s32[1]{0:T(128)}, u32[]{:S(2)}, u32[]{:S(2)}) collective-permute-start(s32[1]{0:T(128)} %bitcast.31), channel_id=1, source_target_pairs={{0,64},{4,68},{8,72},{12,76},{16,80},{20,84},{24,88},{28,92},{32,9... | collective-permute-start | bytes 20 | tf_op jit(solution)/shard_map/while/body/eval_jaxpr/ppermute | solution.py:23
  139.7 4.9 %collective-permute-start = (f32[2,128,64]{2,1,0:T(8,128)S(1)}, f32[2,128,64]{2,1,0:T(8,128)S(1)}, u32[]{:S(2)}, u32[]{:S(2)}) collective-permute-start(f32[2,128,64]{2,1,0:T(8,128)S(1)} %multiply_add_fusion.4), channel_id=1, source_target_pairs={{0,64},{4,68},{8,72},{12,76},{16,80},{20,84},{24,88},{28,92},{32,9... | collective-permute-start | bytes 196616 | tf_op jit(solution)/shard_map/while/body/eval_jaxpr/ppermute | solution.py:23
  145.3 6.0 %collective-permute-start = (f32[2,128,64]{2,1,0:T(8,128)S(1)}, f32[2,128,64]{2,1,0:T(8,128)S(1)}, u32[]{:S(2)}, u32[]{:S(2)}) collective-permute-start(f32[2,128,64]{2,1,0:T(8,128)S(1)} %multiply_add_fusion.4), channel_id=1, source_target_pairs={{0,64},{4,68},{8,72},{12,76},{16,80},{20,84},{24,88},{28,92},{32,9... | collective-permute-start | bytes 196616 | tf_op jit(solution)/shard_map/while/body/eval_jaxpr/ppermute | solution.py:23
  152.1 5.7 %collective-permute-start = (f32[2,128,64]{2,1,0:T(8,128)S(1)}, f32[2,128,64]{2,1,0:T(8,128)S(1)}, u32[]{:S(2)}, u32[]{:S(2)}) collective-permute-start(f32[2,128,64]{2,1,0:T(8,128)S(1)} %multiply_add_fusion.4), channel_id=1, source_target_pairs={{0,64},{4,68},{8,72},{12,76},{16,80},{20,84},{24,88},{28,92},{32,9... | collective-permute-start | bytes 196616 | tf_op jit(solution)/shard_map/while/body/eval_jaxpr/ppermute | solution.py:23
  158.5 5.7 %collective-permute-start = (f32[2,128,64]{2,1,0:T(8,128)S(1)}, f32[2,128,64]{2,1,0:T(8,128)S(1)}, u32[]{:S(2)}, u32[]{:S(2)}) collective-permute-start(f32[2,128,64]{2,1,0:T(8,128)S(1)} %multiply_add_fusion.4), channel_id=1, source_target_pairs={{0,64},{4,68},{8,72},{12,76},{16,80},{20,84},{24,88},{28,92},{32,9... | collective-permute-start | bytes 196616 | tf_op jit(solution)/shard_map/while/body/eval_jaxpr/ppermute | solution.py:23
  165.0 5.7 %collective-permute-start = (f32[2,128,64]{2,1,0:T(8,128)S(1)}, f32[2,128,64]{2,1,0:T(8,128)S(1)}, u32[]{:S(2)}, u32[]{:S(2)}) collective-permute-start(f32[2,128,64]{2,1,0:T(8,128)S(1)} %multiply_add_fusion.4), channel_id=1, source_target_pairs={{0,64},{4,68},{8,72},{12,76},{16,80},{20,84},{24,88},{28,92},{32,9... | collective-permute-start | bytes 196616 | tf_op jit(solution)/shard_map/while/body/eval_jaxpr/ppermute | solution.py:23
  171.4 6.1 %collective-permute-start = (f32[2,128,64]{2,1,0:T(8,128)S(1)}, f32[2,128,64]{2,1,0:T(8,128)S(1)}, u32[]{:S(2)}, u32[]{:S(2)}) collective-permute-start(f32[2,128,64]{2,1,0:T(8,128)S(1)} %multiply_add_fusion.4), channel_id=1, source_target_pairs={{0,64},{4,68},{8,72},{12,76},{16,80},{20,84},{24,88},{28,92},{32,9... | collective-permute-start | bytes 196616 | tf_op jit(solution)/shard_map/while/body/eval_jaxpr/ppermute | solution.py:23
  178.3 7.3 %collective-permute-start = (f32[2,128,64]{2,1,0:T(8,128)S(1)}, f32[2,128,64]{2,1,0:T(8,128)S(1)}, u32[]{:S(2)}, u32[]{:S(2)}) collective-permute-start(f32[2,128,64]{2,1,0:T(8,128)S(1)} %multiply_add_fusion.4), channel_id=1, source_target_pairs={{0,64},{4,68},{8,72},{12,76},{16,80},{20,84},{24,88},{28,92},{32,9... | collective-permute-start | bytes 196616 | tf_op jit(solution)/shard_map/while/body/eval_jaxpr/ppermute | solution.py:23
  186.3 1.0 copy-start.1
  186.8 1.1 copy-start.3
  234.2 1.0 copy-start
  234.3 10.0 %copy-start.5 = (f32[2048]{0:T(1024)S(1)}, f32[2048]{0:T(1024)}, u32[]{:S(2)}) copy-start(f32[2048]{0:T(1024)} %param.25) | copy-start | bytes 24580
where the time goes:
time: 248 us; the launch traced here: 246 us
  starting transfers between devices  81 us (33%)
  waiting for transfers between devices  54.4 us (22%)
  blocking collectives  51.7 us (21%)
  local copies, waits for them, and re-layouts  27.6 us (11%)
  other arithmetic  15.3 us (6%)
  loops' own time  9.07 us (4%)
  matrix products  3.37 us (1%)
  between operations  3.18 us (1%)
    all_to_all x1, blocking collectives, local(): lax.all_to_all(y_send, 'seq', split_axis=0, concat_axis=0, tiled=True)  43.3 us
    ppermute x8, starting transfers between devices, from_behind_2(): return lax.ppermute(value, axis, pairs)  31.1 us
    all_to_all x1, starting transfers between devices, local(): lax.all_to_all(dt_send, 'seq', split_axis=0, concat_axis=0, tiled=True)  18.4 us
    all_to_all x1, waiting for transfers between devices, local(): lax.all_to_all(x_send, 'seq', split_axis=0, concat_axis=0, tiled=True)  17.4 us
    all_to_all x1, waiting for transfers between devices, local(): lax.all_to_all(bc_send, 'seq', split_axis=0, concat_axis=0, tiled=True)  16.5 us
    all_to_all x1, starting transfers between devices, local(): lax.all_to_all(doc_send, 'seq', split_axis=0, concat_axis=0, tiled=True)  11.5 us
    all_to_all x1, waiting for transfers between devices, local(): lax.all_to_all(doc_send, 'seq', split_axis=0, concat_axis=0, tiled=True)  10.8 us
    ppermute x8, waiting for transfers between devices, from_behind_2(): return lax.ppermute(value, axis, pairs)  9.69 us
  transfers between devices with their start and end apart: 15, of which 10 were waited for; matrix products, arithmetic and copies ran while one was open for 15% of the time, Pallas kernels for 0%

commit v1 on v0

v1 whole, which is shorter than its diff:
```python
import jax
import jax.numpy as jnp
from jax import lax
from jax.experimental import pallas as pl
from jax.experimental.pallas import tpu as pltpu
from jax.sharding import PartitionSpec as P

MESH = pl.DeviceIdType.MESH
F32 = jnp.float32
BF16 = jnp.bfloat16

DSTATE = 128
HDIM = 64
SPAN = 256
DI = 8192
EPSILON = 1e-05

RUNS = 16
RUN = 8
HALF = 64
SEGS = 32
SEG = 512
PIECES = 4
WIDTH = 512
LOCAL = 2048
AUX = 384
SLICE = 16


def split(value, parts):
    out = []
    for _ in range(parts):
        piece = value.astype(BF16)
        out.append(piece)
        value = value - piece.astype(F32)
    return jnp.concatenate(out, axis=1)


def dot(a, b, dims=((1,), (0,))):
    return lax.dot_general(a, b, (dims, ((), ())), preferred_element_type=F32)


def silu(u):
    return u * lax.logistic(u)


def body(
    x_hbm,
    aux_hbm,
    z_hbm,
    conv_x,
    bias_x,
    conv_bc,
    bias_bc,
    rate,
    dskip,
    gain,
    out_ref,
    xr,
    ar,
    ext,
    same,
    xc,
    bcc,
    xin,
    xst,
    eout,
    inner,
    srows,
    sbuf,
    srecv,
    inb,
    inr,
    ysend,
    yrecv,
    zbuf,
    part,
    send_sem,
    recv_x,
    recv_a,
    halo_sem,
    state_sem,
    back_sem,
    y_sem,
    part_sem,
    z_sem,
):
    me = lax.axis_index("seq")
    col = lax.axis_index("mp")
    n_col = lax.axis_size("mp")
    half = me // HALF
    t = me % HALF
    q = t // PIECES
    w = t % PIECES
    group = w // 2
    seg = q * 2 + half

    def remote(src, dst, sent, got, seq, mp=col):
        return pltpu.make_async_remote_copy(
            src_ref=src,
            dst_ref=dst,
            send_sem=sent,
            recv_sem=got,
            device_id=(seq, mp),
            device_id_type=MESH,
        )

    def seg_device(r):
        return (r % 2) * HALF + (r // 2) * PIECES + w

    def take(buf, sem):
        pltpu.make_async_copy(buf, buf, sem).wait()

    barrier = pltpu.get_barrier_semaphore()

    @pl.loop(0, HALF - 1)
    def _(k):
        pl.semaphore_signal(
            barrier, inc=1, device_id=(half * HALF + (t + 1 + k) % HALF, col), device_id_type=MESH
        )

    @pl.loop(0, RUNS)
    def _(k):
        pl.semaphore_signal(
            barrier,
            inc=1,
            device_id=((1 - half) * HALF + k * PIECES + w, col),
            device_id_type=MESH,
        )

    for k in range(1, n_col):
        pl.semaphore_signal(
            barrier, inc=1, device_id=(me, (col + k) % n_col), device_id_type=MESH
        )
    pl.semaphore_wait(barrier, HALF - 1 + RUNS + n_col - 1)

    kind = t // 32 + t // 63

    def x_block(d):
        return x_hbm.at[d // PIECES, :, pl.ds(pl.multiple_of((d % PIECES) * WIDTH, 128), WIDTH)]

    def aux_block(d):
        return aux_hbm.at[d // PIECES, (d % PIECES) // 2]

    @pl.loop(1, HALF)
    def _(k):
        d = (t + k) % HALF
        remote(
            aux_block(d), ar.at[1 + t], send_sem.at[1], recv_a.at[kind], half * HALF + d
        ).start()
        remote(x_block(d), xr.at[1 + t], send_sem.at[0], recv_x.at[kind], half * HALF + d).start()

    pltpu.make_async_copy(x_block(t), xr.at[1 + t], recv_x.at[kind]).start()
    pltpu.make_async_copy(aux_block(t), ar.at[1 + t], recv_a.at[kind]).start()
    z_copy = pltpu.make_async_copy(z_hbm, zbuf, z_sem)
    z_copy.start()

    following = seg_device((seg + 1) % SEGS)
    take(xr.at[pl.ds(64, 1)], recv_x.at[2])
    take(ar.at[pl.ds(64, 1)], recv_a.at[2])
    halo_x = remote(xr.at[64], xr.at[0], halo_sem.at[0], halo_sem.at[1], following)
    halo_a = remote(ar.at[64], ar.at[0], halo_sem.at[2], halo_sem.at[3], following)
    halo_x.start()
    halo_a.start()

    lane = lax.broadcasted_iota(jnp.int32, (128, WIDTH), 1)
    row = lax.broadcasted_iota(jnp.int32, (128, WIDTH), 0)
    spread = (row == w * 8 + lax.shift_right_logical(lane, 6)).astype(F32).astype(BF16)
    spread = jnp.concatenate([spread] * 3, axis=0)

    take(ar.at[pl.ds(1, 32)], recv_a.at[0])
    take(ar.at[pl.ds(33, 31)], recv_a.at[1])
    halo_a.wait()

    docs = ar[:, :, 256:384].astype(F32).reshape(SEG + 8, 128)
    docs = jnp.broadcast_to(docs[:, 127:128], (SEG + 8, 128))
    ahead = lax.broadcasted_iota(jnp.int32, (SEG + 8, 128), 0) < 8
    docs = jnp.where(jnp.logical_and(ahead, seg == 0), -1.0, docs)
    ext[...] = docs
    own = ext[8:, :]
    for k in range(1, 4):
        same[k - 1] = (ext[8 - k : 8 - k + SEG, :] == own).astype(F32)
    before = ext[7:8, :]
    last = ext[SEG + 7 : SEG + 8, :]
    from_before = (own == before).astype(F32)
    to_last = (own == last).astype(F32)
    marks = (own == lax.broadcasted_iota(jnp.int32, (SEG, 128), 1).astype(F32)).astype(F32)
    marks = marks.astype(BF16)
    kept = (before == last).astype(F32)

    def conv(block, taps, bias):
        ext[...] = block
        total = bias + taps[3:4] * ext[8:, :]
        for k in range(1, 4):
            total = total + taps[3 - k : 4 - k] * ext[8 - k : 8 - k + SEG, :] * same[k - 1]
        return silu(total).astype(BF16)

    for k in range(2):
        at = pl.ds(pl.multiple_of(k * 256 + group * 128, 128), 128)
        bcc[:, k * 128 : k * 128 + 128] = conv(
            ar[:, :, k * 128 : k * 128 + 128].astype(F32).reshape(SEG + 8, 128),
            conv_bc[:, at],
            bias_bc[:, at],
        )

    raw = ar[1:, :, 256:384].astype(F32).reshape(SEG, 128)
    step = jnp.maximum(raw, 0.0) + jnp.log1p(jnp.exp(-jnp.abs(raw)))
    log_decay = split(-step * rate[...], 3)
    tri = (
        lax.broadcasted_iota(jnp.int32, (SPAN, SPAN), 0)
        >= lax.broadcasted_iota(jnp.int32, (SPAN, SPAN), 1)
    ).astype(F32)
    tri_bf = tri.astype(BF16)
    mids, lasts = [], []
    for c in range(2):
        at = slice(c * SPAN, c * SPAN + SPAN)
        sums = dot(tri_bf, log_decay[at])
        decay = sums[:, :128] + sums[:, 128:256] + sums[:, 256:]
        mid, end = decay[127:128], decay[255:256]
        mids.append(mid)
        lasts.append(end)
        into = jnp.exp(mid - decay) * step[at]
        xin[at] = dot(split(into, 2), spread[:256])
        eout[at] = dot(split(jnp.exp(decay - mid), 2), spread[:256])
    rows = jnp.concatenate(
        [
            jnp.exp(mids[0]),
            jnp.exp(mids[1] + lasts[0] - mids[0]),
            jnp.exp(mids[1] + lasts[0]),
            jnp.exp(lasts[0] - mids[0] + lasts[1]),
            jnp.exp(lasts[1] - mids[1]),
            dskip[...],
            jnp.zeros((2, 128), F32),
        ],
        axis=0,
    )
    srows[...] = dot(split(rows, 3), spread)

    take(xr.at[pl.ds(1, 32)], recv_x.at[0])
    take(xr.at[pl.ds(33, 31)], recv_x.at[1])
    halo_x.wait()

    for j in range(4):
        at = slice(j * 128, j * 128 + 128)
        far = pl.ds(pl.multiple_of(w * WIDTH + j * 128, 128), 128)
        mixed = conv(
            xr[:, :, at].astype(F32).reshape(SEG + 8, 128), conv_x[:, far], bias_x[:, far]
        )
        xc[:, at] = mixed
        scaled = mixed.astype(F32) * xin[:, at]
        xst[:SPAN, at] = (scaled[:SPAN] * srows[3:4, at]).astype(BF16)
        xst[SPAN:, at] = (scaled[SPAN:] * srows[4:5, at]).astype(BF16)
        xin[:, at] = scaled

    weighted = (bcc[:, :128].astype(F32) * to_last).astype(BF16)
    state = dot(xst[...], weighted, ((0,), (0,)))
    passed = jnp.exp(lasts[0] + lasts[1]) * kept
    high = passed.astype(BF16).astype(F32)
    which = lax.broadcasted_iota(jnp.int32, (SLICE, 128), 0)
    tile = jnp.where(which == 0, high, jnp.where(which == 1, passed - high, 0.0))
    sbuf[:, :SLICE] = state.reshape(SEGS, SLICE, 128).astype(BF16)
    sbuf[:, SLICE:] = jnp.broadcast_to(tile.astype(BF16)[None], (SEGS, SLICE, 128))

    @pl.loop(1, SEGS)
    def _(k):
        r = (seg + k) % SEGS
        remote(sbuf.at[r], srecv.at[seg], send_sem.at[2], state_sem, seg_device(r)).start()

    pltpu.make_async_copy(sbuf.at[seg], srecv.at[seg], state_sem).start()

    for c in range(2):
        at = slice(c * SPAN, c * SPAN + SPAN)
        seen = dot(marks[at], marks[at], ((1,), (1,))) * tri
        scores = dot(bcc[at, 128:], bcc[at, :128], ((1,), (1,)))
        total = dot((scores * seen).astype(BF16), xin[at].astype(BF16))
        if c:
            seen = dot(marks[at], marks[:SPAN], ((1,), (1,)))
            scores = dot(bcc[at, 128:], bcc[:SPAN, :128], ((1,), (1,)))
            total = total + dot((scores * seen).astype(BF16), xin[:SPAN].astype(BF16)) * srows[1:2]
        inner[at] = total
    reads = (bcc[:, 128:].astype(F32) * from_before).astype(BF16)

    take(srecv, state_sem)
    head = lax.broadcasted_iota(jnp.int32, (SEGS, 128), 1) == w * 8 + seg // 4
    factor = srecv[:, SLICE : SLICE + 8, :].astype(F32)
    factor = jnp.sum(factor, axis=1)
    factor = jnp.sum(jnp.where(head, factor, 0.0), axis=1, keepdims=True)
    carried = jnp.zeros((SLICE, 128), F32)
    for g in range(SEGS):
        inb[g] = carried.astype(BF16)
        carried = srecv[g, :SLICE, :].astype(F32) + factor[g : g + 1] * carried

    @pl.loop(1, SEGS)
    def _(k):
        r = (seg + k) % SEGS
        remote(inb.at[r], inr.at[seg], send_sem.at[3], back_sem, seg_device(r)).start()

    pltpu.make_async_copy(inb.at[seg], inr.at[seg], back_sem).start()

    z_copy.wait()

    take(inr, back_sem)
    incoming = inr[...].reshape(SEG, 128)

    for c in range(2):
        at = slice(c * SPAN, c * SPAN + SPAN)
        cross = dot(reads[at], incoming, ((1,), (1,))) * srows[2 * c : 2 * c + 1]
        y = (inner[at] + cross) * eout[at] + srows[5:6] * xc[at].astype(F32)
        ysend[c * 32 : c * 32 + 32] = y.reshape(32, RUN, WIDTH).astype(BF16)
        place = yrecv.at[q, :, pl.ds(pl.multiple_of(w * WIDTH, 128), WIDTH)]

        @pl.loop(0, 32)
        def _(k):
            d = c * 32 + (t + k) % 32

            @pl.when(d != t)
            def _():
                remote(ysend.at[d], place, send_sem.at[4], y_sem, half * HALF + d).start()

    pltpu.make_async_copy(
        ysend.at[t], yrecv.at[q, :, pl.ds(pl.multiple_of(w * WIDTH, 128), WIDTH)], y_sem
    ).start()

    take(yrecv, y_sem)
    gated = yrecv[...].astype(F32).reshape(RUNS * RUN, LOCAL) * silu(
        zbuf[...].astype(F32).reshape(RUNS * RUN, LOCAL)
    )
    square = jnp.sum(gated * gated, axis=1, keepdims=True)
    part[col] = jnp.transpose(jnp.broadcast_to(square, (128, 128)))[:8]
    for k in range(1, n_col):
        remote(
            part.at[col], part.at[col], send_sem.at[5], part_sem, me, (col + k) % n_col
        ).start()
    take(part.at[pl.ds(0, n_col - 1)], part_sem)
    total = jnp.sum(part[...], axis=0)
    total = jnp.transpose(jnp.broadcast_to(total[:1], (128, 128)))[:, :1]
    out_ref[...] = (gated * lax.rsqrt(total / DI + EPSILON) * gain[...]).astype(BF16)

    take(xr.at[pl.ds(0, 63)], send_sem.at[0])
    take(ar.at[pl.ds(0, 63)], send_sem.at[1])
    take(sbuf.at[pl.ds(0, 31)], send_sem.at[2])
    take(inb.at[pl.ds(0, 31)], send_sem.at[3])
    take(ysend.at[pl.ds(0, 63)], send_sem.at[4])
    take(part.at[pl.ds(0, n_col - 1)], send_sem.at[5])


def local(
    x_in, bc_in, dt_raw, doc_id, conv_x, bias_x, conv_bc, bias_bc, rate, dskip, z_in, norm_gain
):
    n_col = lax.axis_size("mp")
    rows = x_in.shape[0]
    heads = rate.shape[0]
    bc = bc_in.reshape(RUNS, RUN, 2, 2, DSTATE).transpose(0, 3, 1, 2, 4)
    bc = bc.reshape(RUNS, 2, RUN, 2 * DSTATE)
    tail = jnp.concatenate(
        [dt_raw, jnp.broadcast_to(doc_id.astype(BF16)[:, None], (rows, 128 - heads))], axis=1
    )
    tail = jnp.broadcast_to(tail.reshape(RUNS, 1, RUN, 128), (RUNS, 2, RUN, 128))
    aux = jnp.concatenate([bc, tail], axis=3)
    vmem = pl.BlockSpec(memory_space=pltpu.VMEM)
    anywhere = pl.BlockSpec(memory_space=pl.ANY)
    lanes = [(0, 0), (0, 128 - heads)]
    dma = pltpu.SemaphoreType.DMA
    return pl.pallas_call(
        body,
        out_shape=jax.ShapeDtypeStruct((rows, LOCAL), BF16),
        in_specs=[anywhere] * 3 + [vmem] * 7,
        out_specs=vmem,
        scratch_shapes=[
            pltpu.VMEM((65, RUN, WIDTH), BF16),
            pltpu.VMEM((65, RUN, AUX), BF16),
            pltpu.VMEM((SEG + 8, 128), F32),
            pltpu.VMEM((3, SEG, 128), F32),
            pltpu.VMEM((SEG, WIDTH), BF16),
            pltpu.VMEM((SEG, 256), BF16),
            pltpu.VMEM((SEG, WIDTH), F32),
            pltpu.VMEM((SEG, WIDTH), BF16),
            pltpu.VMEM((SEG, WIDTH), F32),
            pltpu.VMEM((SEG, WIDTH), F32),
            pltpu.VMEM((8, WIDTH), F32),
            pltpu.VMEM((SEGS, 2 * SLICE, 128), BF16),
            pltpu.VMEM((SEGS, 2 * SLICE, 128), BF16),
            pltpu.VMEM((SEGS, SLICE, 128), BF16),
            pltpu.VMEM((SEGS, SLICE, 128), BF16),
            pltpu.VMEM((64, RUN, WIDTH), BF16),
            pltpu.VMEM((RUNS, RUN, LOCAL), BF16),
            pltpu.VMEM((RUNS, RUN, LOCAL), BF16),
            pltpu.VMEM((n_col, 8, 128), F32),
            dma((6,)),
            dma((3,)),
            dma((3,)),
            dma((4,)),
            dma,
            dma,
            dma,
            dma,
            dma,
        ],
        compiler_params=pltpu.CompilerParams(
            collective_id=0, has_side_effects=True, vmem_limit_bytes=40 * 2**20
        ),
    )(
        x_in.reshape(RUNS, RUN, LOCAL),
        aux,
        z_in.reshape(RUNS, RUN, LOCAL),
        conv_x,
        bias_x[None],
        conv_bc.reshape(4, 512),
        bias_bc.reshape(1, 512),
        jnp.pad(rate[None], lanes),
        jnp.pad(dskip[None], lanes),
        norm_gain[None],
    )


def solution(mesh):
    placed = (
        P("seq", "mp"),
        P("seq", None, "mp"),
        P("seq", "mp"),
        P("seq"),
        P(None, "mp"),
        P("mp"),
        P(None, None, "mp"),
        P(None, "mp"),
        P("mp"),
        P("mp"),
        P("seq", "mp"),
        P("mp"),
    )
    return jax.shard_map(
        local, mesh=mesh, in_specs=placed, out_specs=P("seq", "mp"), check_vma=False
    )
```

time: 248 us -> 86.6 us (0.35)
  Pallas kernels: 0 us -> 82.1 us
  starting transfers between devices: 81 us -> 0 us
  waiting for transfers between devices: 54.4 us -> 0 us
  blocking collectives: 51.7 us -> 0 us
  local copies, waits for them, and re-layouts: 27.6 us -> 4.13 us
  other arithmetic: 15.3 us -> 0.11 us
  loops' own time: 9.07 us -> 0 us
  matrix products: 3.37 us -> 0 us
  between operations: 3.18 us -> 0.13 us
    pallas_call x0 -> x1, Pallas kernels: none -> 82.1 us  [local(): pl.pallas_call(body, out_shape=jax.ShapeDtypeStruct((rows, LOCAL), BF16),...]
    all_to_all x4 -> x0, waiting for transfers between devices: 44.7 us -> none  [the longest x1 17.4 us: local(): lax.all_to_all(x_send, 'seq', split_axis=0, concat_axis=0, tiled=True)]
    all_to_all x1 -> x0, blocking collectives: 43.3 us -> none  [local(): lax.all_to_all(y_send, 'seq', split_axis=0, concat_axis=0, tiled=True)]
    all_to_all x4 -> x0, starting transfers between devices: 41 us -> none  [the longest x1 18.4 us: local(): lax.all_to_all(dt_send, 'seq', split_axis=0, concat_axis=0, tiled=True)]
    ppermute x11 -> x0, starting transfers between devices: 40 us -> none  [the longest x8 31.1 us: from_behind_2(): return lax.ppermute(value, axis, pairs)]
    ppermute x11 -> x0, waiting for transfers between devices: 9.7 us -> none  [the longest x8 9.69 us: from_behind_2(): return lax.ppermute(value, axis, pairs)]
    another operation x1 -> x0, loops' own time: 9.07 us -> none  [local(): lax.fori_loop(0, seg_count - 1, advance, jax.tree.map(jnp.zeros_like, seg...]
    psum x1 -> x0, blocking collectives: 8.47 us -> none  [local(): square = lax.psum(jnp.sum(gated * gated, axis=1), 'mp')]
  transfers between devices with their start and end apart: 15 -> 0, of which waited for: 10 -> 0; matrix products, arithmetic and copies ran while one was open for 15% -> 0% of each run, Pallas kernels for 0% -> 0%
where the time goes in v1:
time: 86.6 us; the launch traced here: 86.4 us
  Pallas kernels  82.1 us (95%)
  local copies, waits for them, and re-layouts  4.13 us (5%)
    pallas_call x1, Pallas kernels, local(): pl.pallas_call(body, out_shape=jax.ShapeDtypeStruct((rows, LOCAL), BF16),...  82.1 us
    unnamed x24, local copies, waits for them, and re-layouts  3.92 us

profile of v1, /device:TPU:1, one launch (start us, length us, event | category | flops | bytes accessed | tf_op | source)
XLA Modules:
  0.0 86.4 jit_solution(14637711143202000573)
XLA Ops:
  0.0 0.0 copy-start.9
  0.0 0.0 copy-start.7
  0.0 0.0 copy-start.8
  0.0 0.0 copy-start.6
  0.0 0.0 copy-start.5
  0.0 0.6 copy-done.7
  0.7 0.0 copy-done.8
  0.7 0.0 copy-done.9
  0.7 0.0 copy-done.6
  0.7 0.7 copy.15
  1.4 0.1 broadcast_in_dim.25
  1.5 0.8 copy.14
  2.3 0.0 copy-start.1
  2.3 0.1 maximum_bitcast_fusion
  2.4 0.0 copy-start
  2.5 0.0 copy-done.5
  2.5 0.1 reshape.22
  2.6 0.0 copy-start.2
  2.6 0.0 copy-start.3
  2.6 0.0 copy-start.4
  2.7 0.7 copy-done.1
  3.4 0.2 copy-done
  3.6 0.0 copy-done.2
  3.6 0.0 copy-done.3
  3.6 0.0 copy-done.4
  3.6 82.1 %shard_map.118 = bf16[128,2048]{1,0:T(8,128)(2,1)S(1)} custom-call(bf16[16,8,2048]{2,1,0:T(8,128)(2,1)S(1)} %bitcast.18, bf16[16,2,8,384]{3,2,1,0:T(8,128)(2,1)S(1)} %pad_maximum_fusion.aux_hbm, bf16[16,8,2048]{2,1,0:T(8,128)(2,1)S(1)} %bitcast.19, f32[4,2048]{1,0:T(4,128)S(1)} %copy-done.2, f32[1,2048]{1,0:T(1,128)S(1)} %bitcast.21, f32[4,512]{1,0:T(4,128)S(1)} %bitcast.20, ...), custom_call_target="tpu_custom_call" | custom-call | tf_op jit(solution)/shard_map/pallas_call | solution.py:364
  85.6 0.8 copy.20
  (7 shorter events, 0.1 us)
Async XLA Ops:
  0.0 0.7 copy-start.9
  0.0 0.7 copy-start.7
  0.0 0.7 copy-start.8
  0.0 0.7 copy-start.6
  0.0 2.4 %copy-start.5 = (bf16[128,2,256]{2,1,0:T(2,128)(2,1)S(1)}, bf16[128,2,256]{2,1,0:T(2,128)(2,1)}, u32[]{:S(2)}) copy-start(bf16[128,2,256]{2,1,0:T(2,128)(2,1)} %param.13) | copy-start | bytes 393220
  2.3 1.0 %copy-start.1 = (bf16[128,2048]{1,0:T(8,128)(2,1)S(1)}, bf16[128,2048]{1,0:T(8,128)(2,1)}, u32[]{:S(2)}) copy-start(bf16[128,2048]{1,0:T(8,128)(2,1)} %param.22) | copy-start | bytes 1572868
  2.4 1.1 %copy-start = (bf16[128,2048]{1,0:T(8,128)(2,1)S(1)}, bf16[128,2048]{1,0:T(8,128)(2,1)}, u32[]{:S(2)}) copy-start(bf16[128,2048]{1,0:T(8,128)(2,1)} %param.12) | copy-start | bytes 1572868
  2.6 1.0 %copy-start.2 = (f32[4,2048]{1,0:T(4,128)S(1)}, f32[4,2048]{1,0:T(4,128)}, u32[]{:S(2)}) copy-start(f32[4,2048]{1,0:T(4,128)} %conv_x.1) | copy-start | bytes 98308
  2.6 1.0 %copy-start.3 = (f32[2048]{0:T(1024)S(1)}, f32[2048]{0:T(1024)}, u32[]{:S(2)}) copy-start(f32[2048]{0:T(1024)} %param.17) | copy-start | bytes 24580
  2.6 0.9 %copy-start.4 = (f32[2048]{0:T(1024)S(1)}, f32[2048]{0:T(1024)}, u32[]{:S(2)}) copy-start(f32[2048]{0:T(1024)} %param.23) | copy-start | bytes 24580

commit v2 on v1

v2 whole, which is shorter than its diff:
```python
import jax
import jax.numpy as jnp
from jax import lax
from jax.experimental import pallas as pl
from jax.experimental.pallas import tpu as pltpu
from jax.sharding import PartitionSpec as P

MESH = pl.DeviceIdType.MESH
F32 = jnp.float32
BF16 = jnp.bfloat16

DSTATE = 128
HDIM = 64
SPAN = 256
DI = 8192
EPSILON = 1e-05

RUNS = 16
RUN = 8
HALF = 64
SEGS = 32
SEG = 512
PIECES = 4
WIDTH = 512
LOCAL = 2048
AUX = 384
NB = 1
PART = WIDTH // NB
SLICE = PART // SEGS


def split(value, parts):
    out = []
    for _ in range(parts):
        piece = value.astype(BF16)
        out.append(piece)
        value = value - piece.astype(F32)
    return jnp.concatenate(out, axis=1)


def dot(a, b, dims=((1,), (0,))):
    return lax.dot_general(a, b, (dims, ((), ())), preferred_element_type=F32)


def silu(u):
    return u * lax.logistic(u)


def body(
    x_hbm,
    z_hbm,
    bc_hbm,
    dt_hbm,
    doc_hbm,
    conv_x_hbm,
    bias_x_hbm,
    conv_bc_hbm,
    bias_bc_hbm,
    rate_hbm,
    dskip_hbm,
    gain_hbm,
    out_ref,
    bc_in,
    dt_in,
    doc_in,
    conv_x,
    bias_x,
    conv_bc,
    bias_bc,
    rate,
    dskip,
    gain,
    asend,
    xr,
    ar,
    ext,
    same,
    xc,
    bcc,
    xin,
    xst,
    eout,
    inner,
    srows,
    psend,
    precv,
    sbuf,
    srecv,
    inb,
    inr,
    ysend,
    yrecv,
    zbuf,
    zs,
    part,
    ready_sem,
    send_sem,
    recv_x,
    recv_a,
    share_sem,
    halo_x_sem,
    halo_a_sem,
    pass_sem,
    state_sem,
    back_sem,
    y_sem,
    part_sem,
    z_sem,
    load_sem,
):
    me = lax.axis_index("seq")
    col = lax.axis_index("mp")
    n_col = lax.axis_size("mp")
    half = me // HALF
    t = me % HALF
    q = t // PIECES
    w = t % PIECES
    group = w // 2
    core = t % 2
    chip = t // 2
    seg = q * 2 + half

    def remote(src, dst, sent, got, seq, mp=col):
        return pltpu.make_async_remote_copy(
            src_ref=src,
            dst_ref=dst,
            send_sem=sent,
            recv_sem=got,
            device_id=(seq, mp),
            device_id_type=MESH,
        )

    def signal(sem, seq, mp=col):
        pl.semaphore_signal(sem, inc=1, device_id=(seq, mp), device_id_type=MESH)

    def seg_device(r):
        return (r % 2) * HALF + (r // 2) * PIECES + w

    def take(buf, sem):
        pltpu.make_async_copy(buf, buf, sem).wait()

    loads = [
        pltpu.make_async_copy(src, dst, load_sem.at[k])
        for k, (src, dst) in enumerate(
            [
                (bc_hbm, bc_in),
                (dt_hbm, dt_in),
                (doc_hbm, doc_in),
                (conv_x_hbm, conv_x),
                (bias_x_hbm, bias_x),
                (conv_bc_hbm, conv_bc),
                (bias_bc_hbm, bias_bc),
                (rate_hbm, rate),
                (dskip_hbm, dskip),
                (gain_hbm, gain),
            ]
        )
    ]
    for copy in loads[:3]:
        copy.start()

    barrier = pltpu.get_barrier_semaphore()
    plane, spot = me // 16, me % 16
    for k in range(1, 8):
        signal(barrier, ((plane + k) % 8) * 16 + spot)
    for k in range(1, 16):
        signal(barrier, plane * 16 + (spot + k) % 16)
    for k in range(1, n_col):
        signal(barrier, me, (col + k) % n_col)

    for copy in loads[3:]:
        copy.start()
    z_copy = pltpu.make_async_copy(z_hbm, zbuf, z_sem)
    z_copy.start()
    for copy in loads[:3]:
        copy.wait()

    doc = jnp.broadcast_to(doc_in[...].astype(F32), (128 - 32, 128))
    tail = jnp.transpose(jnp.concatenate([dt_in[...].astype(F32), doc], axis=0))
    tail = tail.reshape(RUNS, RUN, 128).astype(BF16)
    pairs = bc_in[...].astype(F32)
    for k in range(2):
        for n in range(2):
            part_bc = pairs[:, n, k * 128 : k * 128 + 128].astype(BF16)
            asend[:, k, :, n * 128 : n * 128 + 128] = part_bc.reshape(RUNS, RUN, 128)
        asend[:, k, :, 256:] = tail

    pl.semaphore_wait(barrier, 7 + 15 + n_col - 1)
    for k in range(1, 8):
        signal(ready_sem, ((plane + k) % 8) * 16 + spot)
    pl.semaphore_wait(ready_sem, 7)

    kind = t // 63

    def x_block(b, d):
        at = pl.multiple_of((d % PIECES) * WIDTH + b * PART, 128)
        return x_hbm.at[d // PIECES, :, pl.ds(at, PART)]

    def aux_block(d):
        return asend.at[d // PIECES, (d % PIECES) // 2]

    def send_x(b):
        @pl.loop(1, HALF)
        def _(k):
            d = (t + k * 33) % HALF
            remote(
                x_block(b, d), xr.at[b, 1 + t], send_sem.at[0], recv_x.at[b, kind], half * HALF + d
            ).start()

        pltpu.make_async_copy(x_block(b, t), xr.at[b, 1 + t], recv_x.at[b, kind]).start()

    @pl.loop(1, HALF // 2)
    def _(k):
        d = ((chip + k * 17) % 32) * 2 + core
        remote(
            aux_block(d), ar.at[1 + chip, core], send_sem.at[1], recv_a, half * HALF + d
        ).start()

    pltpu.make_async_copy(aux_block(t), ar.at[1 + chip, core], recv_a).start()
    for b in range(NB):
        send_x(b)

    take(ar.at[pl.ds(1, 32), core], recv_a)
    share = remote(
        ar.at[pl.ds(1, 32), core],
        ar.at[pl.ds(1, 32), core],
        share_sem.at[0],
        share_sem.at[1],
        me + 1 - 2 * core,
    )
    share.start()
    share.wait()

    following = seg_device((seg + 1) % SEGS)
    halo_a = remote(ar.at[32, 1], ar.at[0, 1], halo_a_sem.at[0], halo_a_sem.at[1], following)
    halo_a.start()

    def halo_x(b):
        return remote(
            xr.at[b, 64], xr.at[b, 0], halo_x_sem.at[b, 0], halo_x_sem.at[b, 1], following
        )

    for copy in loads[3:]:
        copy.wait()
    none = jnp.zeros((1, 96), F32)
    rates = jnp.concatenate([rate[...], none], axis=1)
    skips = jnp.concatenate([dskip[...], none], axis=1)
    lane = lax.broadcasted_iota(jnp.int32, (128, WIDTH), 1)
    row = lax.broadcasted_iota(jnp.int32, (128, WIDTH), 0)
    spread = (row == w * 8 + lax.shift_right_logical(lane, 6)).astype(F32).astype(BF16)
    spread = jnp.concatenate([spread] * 3, axis=0)

    raw = ar[1:, :, :, 256:384].astype(F32).reshape(SEG, 128)
    step = jnp.maximum(raw, 0.0) + jnp.log1p(jnp.exp(-jnp.abs(raw)))
    log_decay = split(-step * rates, 3)
    tri = (
        lax.broadcasted_iota(jnp.int32, (SPAN, SPAN), 0)
        >= lax.broadcasted_iota(jnp.int32, (SPAN, SPAN), 1)
    ).astype(F32)
    tri_bf = tri.astype(BF16)
    mids, lasts = [], []
    for c in range(2):
        at = slice(c * SPAN, c * SPAN + SPAN)
        sums = dot(tri_bf, log_decay[at])
        decay = sums[:, :128] + sums[:, 128:256] + sums[:, 256:]
        mid, end = decay[127:128], decay[255:256]
        mids.append(mid)
        lasts.append(end)
        into = jnp.exp(mid - decay) * step[at]
        xin[at] = dot(split(into, 2), spread[:256])
        eout[at] = dot(split(jnp.exp(decay - mid), 2), spread[:256])
    rows = jnp.concatenate(
        [
            jnp.exp(mids[0]),
            jnp.exp(mids[1] + lasts[0] - mids[0]),
            jnp.exp(mids[1] + lasts[0]),
            jnp.exp(lasts[0] - mids[0] + lasts[1]),
            jnp.exp(lasts[1] - mids[1]),
            skips,
            jnp.zeros((2, 128), F32),
        ],
        axis=0,
    )
    srows[...] = dot(split(rows, 3), spread)

    take(xr.at[0, pl.ds(64, 1)], recv_x.at[0, 1])
    halo_x(0).start()
    halo_a.wait()

    docs = ar[:, :, :, 256:384].astype(F32).reshape(SEG + 16, 128)[8:]
    docs = jnp.broadcast_to(docs[:, 127:128], (SEG + 8, 128))
    ahead = lax.broadcasted_iota(jnp.int32, (SEG + 8, 128), 0) < 8
    docs = jnp.where(jnp.logical_and(ahead, seg == 0), -1.0, docs)
    ext[...] = docs
    own = ext[8:, :]
    for k in range(1, 4):
        same[k - 1] = (ext[8 - k : 8 - k + SEG, :] == own).astype(F32)
    before = ext[7:8, :]
    last = ext[SEG + 7 : SEG + 8, :]
    from_before = (own == before).astype(F32)
    to_last = (own == last).astype(F32)
    marks = (own == lax.broadcasted_iota(jnp.int32, (SEG, 128), 1).astype(F32)).astype(F32)
    marks = marks.astype(BF16)

    psend[...] = jnp.exp(lasts[0] + lasts[1]) * (before == last).astype(F32)

    @pl.loop(1, SEGS)
    def _(k):
        r = (seg + k * 17) % SEGS
        remote(psend, precv.at[seg], send_sem.at[5], pass_sem, seg_device(r)).start()

    pltpu.make_async_copy(psend, precv.at[seg], pass_sem).start()

    def conv(block, taps, bias):
        ext[...] = block
        total = bias + taps[3:4] * ext[8:, :]
        for k in range(1, 4):
            total = total + taps[3 - k : 4 - k] * ext[8 - k : 8 - k + SEG, :] * same[k - 1]
        return silu(total).astype(BF16)

    for k in range(2):
        at = pl.ds(pl.multiple_of(group * 128, 128), 128)
        block = ar[:, :, :, k * 128 : k * 128 + 128].astype(F32)
        bcc[:, k * 128 : k * 128 + 128] = conv(
            block.reshape(SEG + 16, 128)[8:], conv_bc[:, k, at], bias_bc[k : k + 1, at]
        )
    weighted = (bcc[:, :128].astype(F32) * to_last).astype(BF16)
    reads = (bcc[:, 128:].astype(F32) * from_before).astype(BF16)

    scored = []
    for c, e in ((0, 0), (1, 1), (1, 0)):
        at, to = slice(c * SPAN, c * SPAN + SPAN), slice(e * SPAN, e * SPAN + SPAN)
        seen = dot(marks[at], marks[to], ((1,), (1,)))
        if c == e:
            seen = seen * tri
        scored.append((dot(bcc[at, 128:], bcc[to, :128], ((1,), (1,))) * seen).astype(BF16))

    for b in range(NB):
        here = slice(b * PART, b * PART + PART)
        if b:
            take(xr.at[b, pl.ds(64, 1)], recv_x.at[b, 1])
            halo_x(b).start()
        take(xr.at[b, pl.ds(1, 63)], recv_x.at[b, 0])
        halo_x(b).wait()
        for j in range(PART // 128):
            at = slice(b * PART + j * 128, b * PART + j * 128 + 128)
            far = pl.ds(pl.multiple_of(w * WIDTH + b * PART + j * 128, 128), 128)
            mixed = conv(
                xr[b, :, :, j * 128 : j * 128 + 128].astype(F32).reshape(SEG + 8, 128),
                conv_x[:, far],
                bias_x[:, far],
            )
            xc[:, at] = mixed
            scaled = mixed.astype(F32) * xin[:, at]
            xst[:SPAN, at] = (scaled[:SPAN] * srows[3:4, at]).astype(BF16)
            xst[SPAN:, at] = (scaled[SPAN:] * srows[4:5, at]).astype(BF16)
            xin[:, at] = scaled
        state = dot(xst[:, here], weighted, ((0,), (0,)))
        sbuf[b] = state.reshape(SEGS, SLICE, 128).astype(BF16)

        @pl.loop(1, SEGS)
        def _(k):
            r = (seg + k * 17) % SEGS
            remote(
                sbuf.at[b, r], srecv.at[b, seg], send_sem.at[2], state_sem.at[b], seg_device(r)
            ).start()

        pltpu.make_async_copy(sbuf.at[b, seg], srecv.at[b, seg], state_sem.at[b]).start()

        inner[:SPAN, here] = dot(scored[0], xin[:SPAN, here].astype(BF16))
        inner[SPAN:, here] = (
            dot(scored[1], xin[SPAN:, here].astype(BF16))
            + dot(scored[2], xin[:SPAN, here].astype(BF16)) * srows[1:2, here]
        )

    z_copy.wait()
    for k in range(RUNS):
        zs[k * RUN : k * RUN + RUN] = silu(zbuf[k].astype(F32))

    take(precv, pass_sem)
    factors = precv[...].reshape(SEGS, 128)
    lanes = lax.broadcasted_iota(jnp.int32, (SEGS, 128), 1)
    for b in range(NB):
        head = lanes == w * 8 + b * (8 // NB) + seg * SLICE // HDIM
        factor = jnp.sum(jnp.where(head, factors, 0.0), axis=1, keepdims=True)
        take(srecv.at[b], state_sem.at[b])
        carried = jnp.zeros((SLICE, 128), F32)
        for g in range(SEGS):
            inb[b, g] = carried.astype(BF16)
            carried = srecv[b, g].astype(F32) + factor[g : g + 1] * carried

        @pl.loop(1, SEGS)
        def _(k):
            r = (seg + k * 17) % SEGS
            remote(
                inb.at[b, r], inr.at[b, seg], send_sem.at[3], back_sem.at[b], seg_device(r)
            ).start()

        pltpu.make_async_copy(inb.at[b, seg], inr.at[b, seg], back_sem.at[b]).start()

    for b in range(NB):
        here = slice(b * PART, b * PART + PART)
        take(inr.at[b], back_sem.at[b])
        incoming = inr[b].astype(F32).reshape(PART, 128).astype(BF16)
        for c in range(2):
            at = slice(c * SPAN, c * SPAN + SPAN)
            cross = dot(reads[at], incoming, ((1,), (1,))) * srows[2 * c : 2 * c + 1, here]
            y = (inner[at, here] + cross) * eout[at, here]
            y = y + srows[5:6, here] * xc[at, here].astype(F32)
            ysend[b, c * 32 : c * 32 + 32] = y.reshape(32, RUN, PART).astype(BF16)
        place = yrecv.at[b, q, :, pl.ds(pl.multiple_of(w * PART, 128), PART)]

        @pl.loop(1, HALF)
        def _(k):
            d = (t + k * 33) % HALF
            remote(ysend.at[b, d], place, send_sem.at[4], y_sem.at[b], half * HALF + d).start()

        pltpu.make_async_copy(ysend.at[b, t], place, y_sem.at[b]).start()

    sums = jnp.zeros((RUNS * RUN, PART), F32)
    for b in range(NB):
        take(yrecv.at[b], y_sem.at[b])
        for k in range(PIECES):
            at = slice(k * WIDTH + b * PART, k * WIDTH + b * PART + PART)
            y = yrecv[b, :, :, k * PART : k * PART + PART].astype(F32)
            gated = y.reshape(RUNS * RUN, PART) * zs[:, at]
            zs[:, at] = gated
            sums = sums + gated * gated
    square = jnp.sum(sums, axis=1, keepdims=True)
    part[col] = jnp.transpose(jnp.broadcast_to(square, (128, 128)))[:8]
    for k in range(1, n_col):
        remote(
            part.at[col], part.at[col], send_sem.at[6], part_sem, me, (col + k) % n_col
        ).start()
    take(part.at[pl.ds(0, n_col - 1)], part_sem)
    total = jnp.sum(part[...], axis=0)
    total = jnp.transpose(jnp.broadcast_to(total[:1], (128, 128)))[:, :1]
    scale = lax.rsqrt(total / DI + EPSILON)
    for k in range(LOCAL // 512):
        at = slice(k * 512, k * 512 + 512)
        out_ref[:, at] = (zs[:, at] * scale * gain[:, at]).astype(BF16)

    for b in range(NB):
        take(xr.at[b, pl.ds(0, 63)], send_sem.at[0])
        take(sbuf.at[b, pl.ds(0, 31)], send_sem.at[2])
        take(inb.at[b, pl.ds(0, 31)], send_sem.at[3])
        take(ysend.at[b, pl.ds(0, 63)], send_sem.at[4])
    take(ar.at[pl.ds(0, 31), 0], send_sem.at[1])
    take(precv.at[pl.ds(0, 31)], send_sem.at[5])
    take(part.at[pl.ds(0, n_col - 1)], send_sem.at[6])


def local(
    x_in, bc_in, dt_raw, doc_id, conv_x, bias_x, conv_bc, bias_bc, rate, dskip, z_in, norm_gain
):
    n_col = lax.axis_size("mp")
    rows = x_in.shape[0]
    heads = rate.shape[0]
    vmem = pl.BlockSpec(memory_space=pltpu.VMEM)
    hbm = pl.BlockSpec(memory_space=pltpu.HBM)
    dma = pltpu.SemaphoreType.DMA
    return pl.pallas_call(
        body,
        out_shape=jax.ShapeDtypeStruct((rows, LOCAL), BF16),
        in_specs=[hbm] * 12,
        out_specs=vmem,
        scratch_shapes=[
            pltpu.VMEM((rows, 2, 256), BF16),
            pltpu.VMEM((heads, rows), BF16),
            pltpu.VMEM((1, rows), jnp.int32),
            pltpu.VMEM((4, LOCAL), F32),
            pltpu.VMEM((1, LOCAL), F32),
            pltpu.VMEM((4, 2, 256), F32),
            pltpu.VMEM((2, 256), F32),
            pltpu.VMEM((1, heads), F32),
            pltpu.VMEM((1, heads), F32),
            pltpu.VMEM((1, LOCAL), F32),
            pltpu.VMEM((RUNS, 2, RUN, AUX), BF16),
            pltpu.VMEM((NB, 65, RUN, PART), BF16),
            pltpu.VMEM((33, 2, RUN, AUX), BF16),
            pltpu.VMEM((SEG + 8, 128), F32),
            pltpu.VMEM((3, SEG, 128), F32),
            pltpu.VMEM((SEG, WIDTH), BF16),
            pltpu.VMEM((SEG, 256), BF16),
            pltpu.VMEM((SEG, WIDTH), F32),
            pltpu.VMEM((SEG, WIDTH), BF16),
            pltpu.VMEM((SEG, WIDTH), F32),
            pltpu.VMEM((SEG, WIDTH), F32),
            pltpu.VMEM((8, WIDTH), F32),
            pltpu.VMEM((1, 128), F32),
            pltpu.VMEM((SEGS, 1, 128), F32),
            pltpu.VMEM((NB, SEGS, SLICE, 128), BF16),
            pltpu.VMEM((NB, SEGS, SLICE, 128), BF16),
            pltpu.VMEM((NB, SEGS, SLICE, 128), BF16),
            pltpu.VMEM((NB, SEGS, SLICE, 128), BF16),
            pltpu.VMEM((NB, 64, RUN, PART), BF16),
            pltpu.VMEM((NB, RUNS, RUN, PIECES * PART), BF16),
            pltpu.VMEM((RUNS, RUN, LOCAL), BF16),
            pltpu.VMEM((RUNS * RUN, LOCAL), F32),
            pltpu.VMEM((n_col, 8, 128), F32),
            pltpu.SemaphoreType.REGULAR,
            dma((7,)),
            dma((NB, 2)),
            dma,
            dma((2,)),
            dma((NB, 2)),
            dma((2,)),
            dma,
            dma((NB,)),
            dma((NB,)),
            dma((NB,)),
            dma,
            dma,
            dma((10,)),
        ],
        compiler_params=pltpu.CompilerParams(
            collective_id=0, has_side_effects=True, vmem_limit_bytes=60 * 2**20
        ),
    )(
        x_in.reshape(RUNS, RUN, LOCAL),
        z_in.reshape(RUNS, RUN, LOCAL),
        bc_in,
        dt_raw.T,
        doc_id[None],
        conv_x,
        bias_x[None],
        conv_bc,
        bias_bc,
        rate[None],
        dskip[None],
        norm_gain[None],
    )


def solution(mesh):
    placed = (
        P("seq", "mp"),
        P("seq", None, "mp"),
        P("seq", "mp"),
        P("seq"),
        P(None, "mp"),
        P("mp"),
        P(None, None, "mp"),
        P(None, "mp"),
        P("mp"),
        P("mp"),
        P("seq", "mp"),
        P("mp"),
    )
    return jax.shard_map(
        local, mesh=mesh, in_specs=placed, out_specs=P("seq", "mp"), check_vma=False
    )
```

time: 86.6 us -> 75 us (0.87)
  Pallas kernels: 82.1 us -> 73 us
  local copies, waits for them, and re-layouts: 4.13 us -> 1.88 us
    pallas_call x1, Pallas kernels: 82.1 us -> 73 us  [local(): pl.pallas_call(body, out_shape=jax.ShapeDtypeStruct((rows, LOCAL), BF16),...]
    unnamed x24 -> x1, local copies, waits for them, and re-layouts: 3.92 us -> 1.88 us
where the time goes in v2:
time: 75 us; the launch traced here: 74.8 us
  Pallas kernels  73 us (97%)
  local copies, waits for them, and re-layouts  1.88 us (3%)
    pallas_call x1, Pallas kernels, local(): pl.pallas_call(body, out_shape=jax.ShapeDtypeStruct((rows, LOCAL), BF16),...  73 us
    unnamed x1, local copies, waits for them, and re-layouts  1.88 us

profile of v2, /device:TPU:1, one launch (start us, length us, event | category | flops | bytes accessed | tf_op | source)
XLA Modules:
  0.0 74.8 jit_solution(6239460641239147834)
XLA Ops:
  0.0 73.0 %shard_map.118 = bf16[128,2048]{1,0:T(8,128)(2,1)} custom-call(bf16[16,8,2048]{2,1,0:T(8,128)(2,1)} %bitcast.8, bf16[16,8,2048]{2,1,0:T(8,128)(2,1)} %bitcast.9, bf16[128,2,256]{2,1,0:T(2,128)(2,1)} %bc_hbm.1, bf16[32,128]{1,0:T(8,128)(2,1)} %bitcast.10, s32[1,128]{1,0:T(1,128)} %bitcast.13, f32[4,2048]{1,0:T(4,128)} %conv_x_hbm.1, f32[1,2048]{1,0:T(1,128)} %bitcast.11, ...), custom_call_target="tpu_custom_call" | custom-call | tf_op jit(solution)/shard_map/pallas_call | solution.py:462
  73.0 1.9 %copy.14 = bf16[128,2048]{1,0:T(8,128)(2,1)} copy(bf16[128,2048]{1,0:T(8,128)(2,1)} %shard_map.118) | data formatting | bytes 1048576

commit v3 on v2

--- a/solution.py
+++ b/solution.py
@@ -24,9 +24,10 @@
 WIDTH = 512
 LOCAL = 2048
 AUX = 384
-NB = 1
+NB = 2
 PART = WIDTH // NB
 SLICE = PART // SEGS
+CUTS = (24, 64)
 
 
 def split(value, parts):
@@ -172,6 +173,10 @@
         copy.start()
     z_copy = pltpu.make_async_copy(z_hbm, zbuf, z_sem)
     z_copy.start()
+    pl.semaphore_wait(barrier, 7 + 15 + n_col - 1)
+    for k in range(1, 8):
+        signal(ready_sem, ((plane + k) % 8) * 16 + spot)
+
     for copy in loads[:3]:
         copy.wait()
 
@@ -185,9 +190,6 @@
             asend[:, k, :, n * 128 : n * 128 + 128] = part_bc.reshape(RUNS, RUN, 128)
         asend[:, k, :, 256:] = tail
 
-    pl.semaphore_wait(barrier, 7 + 15 + n_col - 1)
-    for k in range(1, 8):
-        signal(ready_sem, ((plane + k) % 8) * 16 + spot)
     pl.semaphore_wait(ready_sem, 7)
 
     kind = t // 63
@@ -199,15 +201,16 @@
     def aux_block(d):
         return asend.at[d // PIECES, (d % PIECES) // 2]
 
-    def send_x(b):
-        @pl.loop(1, HALF)
+    def send_x(b, first, stop):
+        @pl.loop(first, stop)
         def _(k):
-            d = (t + k * 33) % HALF
+            d = (t + k * 37) % HALF
             remote(
                 x_block(b, d), xr.at[b, 1 + t], send_sem.at[0], recv_x.at[b, kind], half * HALF + d
             ).start()
 
-        pltpu.make_async_copy(x_block(b, t), xr.at[b, 1 + t], recv_x.at[b, kind]).start()
+        if first == 1:
+            pltpu.make_async_copy(x_block(b, t), xr.at[b, 1 + t], recv_x.at[b, kind]).start()
 
     @pl.loop(1, HALF // 2)
     def _(k):
@@ -217,8 +220,12 @@
         ).start()
 
     pltpu.make_async_copy(aux_block(t), ar.at[1 + chip, core], recv_a).start()
-    for b in range(NB):
-        send_x(b)
+    send_x(0, 1, CUTS[0])
+
+    z_copy.wait()
+    for k in range(RUNS):
+        zs[k * RUN : k * RUN + RUN] = silu(zbuf[k].astype(F32))
+    send_x(0, CUTS[0], CUTS[1])
 
     take(ar.at[pl.ds(1, 32), core], recv_a)
     share = remote(
@@ -229,6 +236,10 @@
         me + 1 - 2 * core,
     )
     share.start()
+    if CUTS[1] < HALF:
+        send_x(0, CUTS[1], HALF)
+    for b in range(1, NB):
+        send_x(b, 1, HALF // 2)
     share.wait()
 
     following = seg_device((seg + 1) % SEGS)
@@ -285,6 +296,8 @@
 
     take(xr.at[0, pl.ds(64, 1)], recv_x.at[0, 1])
     halo_x(0).start()
+    for b in range(1, NB):
+        send_x(b, HALF // 2, HALF)
     halo_a.wait()
 
     docs = ar[:, :, :, 256:384].astype(F32).reshape(SEG + 16, 128)[8:]
@@ -312,10 +325,12 @@
     pltpu.make_async_copy(psend, precv.at[seg], pass_sem).start()
 
     def conv(block, taps, bias):
-        ext[...] = block
-        total = bias + taps[3:4] * ext[8:, :]
+        size = block.shape[0] - 8
+        ext[: size + 8] = block
+        total = bias + taps[3:4] * block[8:]
         for k in range(1, 4):
-            total = total + taps[3 - k : 4 - k] * ext[8 - k : 8 - k + SEG, :] * same[k - 1]
+            moved = ext[8 - k : 8 - k + size, :] * same[k - 1, :size]
+            total = total + taps[3 - k : 4 - k] * moved
         return silu(total).astype(BF16)
 
     for k in range(2):
@@ -337,24 +352,32 @@
 
     for b in range(NB):
         here = slice(b * PART, b * PART + PART)
-        if b:
-            take(xr.at[b, pl.ds(64, 1)], recv_x.at[b, 1])
-            halo_x(b).start()
         take(xr.at[b, pl.ds(1, 63)], recv_x.at[b, 0])
-        halo_x(b).wait()
+        into = xin[:16, here]
         for j in range(PART // 128):
             at = slice(b * PART + j * 128, b * PART + j * 128 + 128)
             far = pl.ds(pl.multiple_of(w * WIDTH + b * PART + j * 128, 128), 128)
-            mixed = conv(
-                xr[b, :, :, j * 128 : j * 128 + 128].astype(F32).reshape(SEG + 8, 128),
-                conv_x[:, far],
-                bias_x[:, far],
-            )
+            block = xr[b, 1:, :, j * 128 : j * 128 + 128].astype(F32).reshape(SEG, 128)
+            block = jnp.concatenate([jnp.zeros((8, 128), F32), block], axis=0)
+            mixed = conv(block, conv_x[:, far], bias_x[:, far])
             xc[:, at] = mixed
             scaled = mixed.astype(F32) * xin[:, at]
             xst[:SPAN, at] = (scaled[:SPAN] * srows[3:4, at]).astype(BF16)
             xst[SPAN:, at] = (scaled[SPAN:] * srows[4:5, at]).astype(BF16)
             xin[:, at] = scaled
+        if b + 1 < NB:
+            take(xr.at[b + 1, pl.ds(64, 1)], recv_x.at[b + 1, 1])
+            halo_x(b + 1).start()
+        halo_x(b).wait()
+        for j in range(PART // 128):
+            at = slice(b * PART + j * 128, b * PART + j * 128 + 128)
+            far = pl.ds(pl.multiple_of(w * WIDTH + b * PART + j * 128, 128), 128)
+            block = xr[b, :3, :, j * 128 : j * 128 + 128].astype(F32).reshape(24, 128)
+            mixed = conv(block, conv_x[:, far], bias_x[:, far])
+            xc[:16, at] = mixed
+            scaled = mixed.astype(F32) * into[:, j * 128 : j * 128 + 128]
+            xst[:16, at] = (scaled * srows[3:4, at]).astype(BF16)
+            xin[:16, at] = scaled
         state = dot(xst[:, here], weighted, ((0,), (0,)))
         sbuf[b] = state.reshape(SEGS, SLICE, 128).astype(BF16)
 
@@ -372,10 +395,6 @@
             dot(scored[1], xin[SPAN:, here].astype(BF16))
             + dot(scored[2], xin[:SPAN, here].astype(BF16)) * srows[1:2, here]
         )
-
-    z_copy.wait()
-    for k in range(RUNS):
-        zs[k * RUN : k * RUN + RUN] = silu(zbuf[k].astype(F32))
 
     take(precv, pass_sem)
     factors = precv[...].reshape(SEGS, 128)
@@ -412,7 +431,7 @@
 
         @pl.loop(1, HALF)
         def _(k):
-            d = (t + k * 33) % HALF
+            d = (t + k * 37) % HALF
             remote(ysend.at[b, d], place, send_sem.at[4], y_sem.at[b], half * HALF + d).start()
 
         pltpu.make_async_copy(ysend.at[b, t], place, y_sem.at[b]).start()

time: 75 us -> 73.2 us (0.976)
  Pallas kernels: 73 us -> 71.2 us
    pallas_call x1, Pallas kernels: 73 us -> 71.2 us  [local(): pl.pallas_call(body, out_shape=jax.ShapeDtypeStruct((rows, LOCAL), BF16),...]
where the time goes in v3:
time: 73.2 us; the launch traced here: 73 us
  Pallas kernels  71.2 us (97%)
  local copies, waits for them, and re-layouts  1.88 us (3%)
    pallas_call x1, Pallas kernels, local(): pl.pallas_call(body, out_shape=jax.ShapeDtypeStruct((rows, LOCAL), BF16),...  71.2 us
    unnamed x1, local copies, waits for them, and re-layouts  1.88 us

profile of v3, /device:TPU:1, one launch (start us, length us, event | category | flops | bytes accessed | tf_op | source)
XLA Modules:
  0.0 73.0 jit_solution(6237739950369090878)
XLA Ops:
  0.0 71.2 %shard_map.118 = bf16[128,2048]{1,0:T(8,128)(2,1)} custom-call(bf16[16,8,2048]{2,1,0:T(8,128)(2,1)} %bitcast.8, bf16[16,8,2048]{2,1,0:T(8,128)(2,1)} %bitcast.9, bf16[128,2,256]{2,1,0:T(2,128)(2,1)} %bc_hbm.1, bf16[32,128]{1,0:T(8,128)(2,1)} %bitcast.10, s32[1,128]{1,0:T(1,128)} %bitcast.13, f32[4,2048]{1,0:T(4,128)} %conv_x_hbm.1, f32[1,2048]{1,0:T(1,128)} %bitcast.11, ...), custom_call_target="tpu_custom_call" | custom-call | tf_op jit(solution)/shard_map/pallas_call | solution.py:481
  71.2 1.9 %copy.14 = bf16[128,2048]{1,0:T(8,128)(2,1)} copy(bf16[128,2048]{1,0:T(8,128)(2,1)} %shard_map.118) | data formatting | bytes 1048576

commit v4 on v3

--- a/solution.py
+++ b/solution.py
@@ -114,8 +114,10 @@
     n_col = lax.axis_size("mp")
     half = me // HALF
     t = me % HALF
-    q = t // PIECES
-    w = t % PIECES
+    flip = 48 * half
+    role = t ^ flip
+    q = role // PIECES
+    w = role % PIECES
     group = w // 2
     core = t % 2
     chip = t // 2
@@ -135,7 +137,7 @@
         pl.semaphore_signal(sem, inc=1, device_id=(seq, mp), device_id_type=MESH)
 
     def seg_device(r):
-        return (r % 2) * HALF + (r // 2) * PIECES + w
+        return (r % 2) * HALF + (((r // 2) * PIECES + w) ^ (48 * (r % 2)))
 
     def take(buf, sem):
         pltpu.make_async_copy(buf, buf, sem).wait()
@@ -204,22 +206,22 @@
     def send_x(b, first, stop):
         @pl.loop(first, stop)
         def _(k):
-            d = (t + k * 37) % HALF
+            d = (role + k * 37) % HALF
             remote(
-                x_block(b, d), xr.at[b, 1 + t], send_sem.at[0], recv_x.at[b, kind], half * HALF + d
+                x_block(b, d), xr.at[b, 1 + t], send_sem.at[0], recv_x.at[b, kind], half * HALF + (d ^ flip)
             ).start()
 
         if first == 1:
-            pltpu.make_async_copy(x_block(b, t), xr.at[b, 1 + t], recv_x.at[b, kind]).start()
+            pltpu.make_async_copy(x_block(b, role), xr.at[b, 1 + t], recv_x.at[b, kind]).start()
 
     @pl.loop(1, HALF // 2)
     def _(k):
-        d = ((chip + k * 17) % 32) * 2 + core
+        d = ((role // 2 + k * 17) % 32) * 2 + core
         remote(
-            aux_block(d), ar.at[1 + chip, core], send_sem.at[1], recv_a, half * HALF + d
+            aux_block(d), ar.at[1 + chip, core], send_sem.at[1], recv_a, half * HALF + (d ^ flip)
         ).start()
 
-    pltpu.make_async_copy(aux_block(t), ar.at[1 + chip, core], recv_a).start()
+    pltpu.make_async_copy(aux_block(role), ar.at[1 + chip, core], recv_a).start()
     send_x(0, 1, CUTS[0])
 
     z_copy.wait()

time: 73.2 us -> 72.6 us (level)
  no operation moved by 1% of the time
where the time goes in v4:
time: 72.6 us; the launch traced here: 72.4 us
  Pallas kernels  70.5 us (97%)
  local copies, waits for them, and re-layouts  1.88 us (3%)
    pallas_call x1, Pallas kernels, local(): pl.pallas_call(body, out_shape=jax.ShapeDtypeStruct((rows, LOCAL), BF16),...  70.5 us
    unnamed x1, local copies, waits for them, and re-layouts  1.88 us

profile of v4, /device:TPU:1, one launch (start us, length us, event | category | flops | bytes accessed | tf_op | source)
XLA Modules:
  0.0 72.4 jit_solution(16642762663233805736)
XLA Ops:
  0.0 70.5 %shard_map.118 = bf16[128,2048]{1,0:T(8,128)(2,1)} custom-call(bf16[16,8,2048]{2,1,0:T(8,128)(2,1)} %bitcast.8, bf16[16,8,2048]{2,1,0:T(8,128)(2,1)} %bitcast.9, bf16[128,2,256]{2,1,0:T(2,128)(2,1)} %bc_hbm.1, bf16[32,128]{1,0:T(8,128)(2,1)} %bitcast.10, s32[1,128]{1,0:T(1,128)} %bitcast.13, f32[4,2048]{1,0:T(4,128)} %conv_x_hbm.1, f32[1,2048]{1,0:T(1,128)} %bitcast.11, ...), custom_call_target="tpu_custom_call" | custom-call | tf_op jit(solution)/shard_map/pallas_call | solution.py:483
  70.5 1.9 %copy.14 = bf16[128,2048]{1,0:T(8,128)(2,1)} copy(bf16[128,2048]{1,0:T(8,128)(2,1)} %shard_map.118) | data formatting | bytes 1048576
